TPU v7x, 768 devices: a whole 4x8x12 slice. The times are simulated.
768 devices in a mesh: rep: 96 (over z, x, core), fsdp: 8 (over y).
Axes of the slice: x: 4, y: 8, z: 12, core: 2. Of those that a mesh axis runs over, the one named last changes fastest.
Arguments:
- grads: bfloat16 [96, 8, 128, 6144], P('rep', 'fsdp'), may hold values from -4 to 4
- momentum: float32 [96, 128, 6144], P('rep', None, 'fsdp'), may hold values from -6 to 6
- indices: int32 [96, 2, 96, 32], P(None, None, 'fsdp'), may hold values from 0 to 4095, as said below
Outputs:
- new_momentum: float32 [96, 128, 6144], P('rep', None, 'fsdp')
- update: float32 [128, 6144], P(None, 'fsdp')
Inputs may be any that keep to these rules, and one draw needn't show every extreme that they name: `indices`: within each block the 32 positions are distinct, and position k lies in [k * 64 * 2, (k + 1) * 64 * 2). The positions are fixed in advance and known to every replica (they stand in for DeMo's top-k choice, which is not part of this step).
All inputs are finite; a program needn't handle non-finite values.
Results may differ from a plain program's by a relative error of at most 0.0003.
Values sent between devices are 32-bit elements; how exact they have to be, the bound alone decides.
A program may use at most 32 MiB of HBM per device.

v0:
```python
import jax
import jax.numpy as jnp
from jax import lax
from jax.sharding import PartitionSpec as P

SPAN = 64
KEEP = 32


decay_rate = 0.999


def cosine_table():
    freq = jnp.arange(SPAN, dtype=jnp.float32)[:, None]
    sample = jnp.arange(SPAN, dtype=jnp.float32)[None, :]
    table = jnp.cos(jnp.pi * (2.0 * sample + 1.0) * freq / (2.0 * SPAN))
    scales = jnp.where(freq == 0, jnp.sqrt(1.0 / SPAN), jnp.sqrt(2.0 / SPAN))
    return table * scales


def to_blocks(matrix):
    height, width = matrix.shape
    return matrix.reshape(height // SPAN, SPAN, width // SPAN, SPAN).transpose(0, 2, 1, 3)


def from_blocks(blocks):
    bands, groups = (blocks.shape[0], blocks.shape[1])
    return blocks.transpose(0, 2, 1, 3).reshape(bands * SPAN, groups * SPAN)


def forward_transform(matrix, table):
    blocks = to_blocks(matrix)
    spectra = jnp.einsum("ij,acjk,lk->acil", table, blocks, table, precision=lax.Precision.HIGHEST)
    return spectra.reshape(spectra.shape[0], spectra.shape[1], SPAN * SPAN)


def inverse_transform(flat, table):
    spectra = flat.reshape(flat.shape[0], flat.shape[1], SPAN, SPAN)
    blocks = jnp.einsum("ij,acil,lk->acjk", table, spectra, table, precision=lax.Precision.HIGHEST)
    return from_blocks(blocks)


def slot_offsets(positions):
    spacing = SPAN * SPAN // KEEP
    starts = jnp.arange(KEEP, dtype=jnp.int32) * spacing
    return positions - starts


def slot_matches(positions):
    spacing = SPAN * SPAN // KEEP
    within = lax.broadcasted_iota(jnp.int32, (KEEP, spacing), 1)
    return within == slot_offsets(positions)[..., None]


def shards(grads, momentum, indices):
    table = cosine_table()
    spacing = SPAN * SPAN // KEEP
    summed = lax.psum_scatter(grads.astype(jnp.float32), "fsdp", scatter_dimension=3, tiled=True)
    fresh = decay_rate * momentum[0] + summed[0, 0]
    spectra = forward_transform(fresh, table)
    bands, groups = (spectra.shape[0], spectra.shape[1])
    slotted = spectra.reshape(bands, groups, KEEP, spacing)
    replica = lax.axis_index("rep")
    own_positions = lax.dynamic_index_in_dim(indices, replica, 0, keepdims=False)
    matches = slot_matches(own_positions)
    kept = jnp.sum(jnp.where(matches, slotted, 0.0), axis=3)
    own_slotted = jnp.where(matches, kept[..., None], 0.0)
    own = own_slotted.reshape(bands, groups, SPAN * SPAN)
    remaining = fresh - inverse_transform(own, table)
    placed = jnp.where(
        slot_matches(indices), lax.all_gather(kept[None], "rep", axis=0, tiled=True)[..., None], 0.0
    )
    gathered = jnp.sum(placed, axis=0)
    total = gathered.reshape(bands, groups, SPAN * SPAN)
    update = inverse_transform(total, table)
    return (remaining[None], update)


def solution(mesh):
    in_specs = (P("rep", "fsdp", None, None), P("rep", None, "fsdp"), P(None, None, "fsdp", None))
    out_specs = (P("rep", None, "fsdp"), P(None, "fsdp"))
    return jax.shard_map(shards, mesh=mesh, in_specs=in_specs, out_specs=out_specs, check_vma=False)
```

profile of v0, /device:TPU:1, one launch (start us, length us, event | category | flops | bytes accessed | tf_op | source)
XLA Modules:
  0.0 195.6 jit_solution(4702262151959665508)
XLA Ops:
  7.2 1.9 copy.73
  9.1 1.9 convert_element_type.3
  11.0 0.2 copy.72
  11.3 0.5 mul.141
  11.7 0.3 copy-done
  12.0 0.2 constant_dynamic-slice_fusion
  12.2 0.2 copy.75
  12.4 0.1 copy.76
  12.7 0.7 copy.74
  13.4 0.1 broadcast_subtract_fusion
  13.5 1.4 copy.83
  14.9 0.5 compare_select_fusion.2
  15.4 52.5 %reduce-scatter.2.cloned.1.call-done = f32[1,1,128,768]{2,3,1,0:T(8,128)} async-done(((f32[1,1,128,6144]{2,3,1,0:T(8,128)}), f32[1,1,128,768]{2,3,1,0:T(8,128)}) %reduce-scatter.2.cloned.1.call-update) | async-done | bytes 393232 | tf_op jit(solution)/shard_map/reduce_scatter | solution.py:58
  67.9 1.5 squeeze.12
  69.4 0.4 add_bitcast_fusion
  69.8 1.5 fusion.2
  71.3 1.0 fusion
  72.3 0.1 copy.79
  72.5 0.7 copy.84
  73.3 3.3 %fusion.1 = f32[2,12,64,64]{2,3,1,0:T(8,128)S(1)} fusion(f32[2,12,64]{2,1,0:T(8,128)S(1)} %copy.80, s32[2,12,64]{2,1,0:T(8,128)S(1)} %copy.77, s32[64,64]{0,1:T(8,128)} %copy.74, f32[64]{0:T(128)} %get-tuple-element.12, f32[64]{0:T(128)} %get-tuple-element.13), kind=kOutput, calls=%fused_computation.7 | convolution fusion | flops 75706368 | bytes 422400 | tf_op jit(solution)/shard_map/ij,acil,lk->acjk/dot_general | solution.py:39
  76.6 1.5 convolution_bitcast_fusion.1
  78.1 0.5 copy.82
  78.6 0.4 reshape.55
  79.0 1.1 fusion.4
  80.1 0.9 copy.88
  81.0 81.5 %all-gather = f32[192,12,32]{2,1,0:T(8,128)S(1)} all-gather(f32[2,12,32]{2,1,0:T(8,128)S(1)} %copy-done.3), channel_id=2, replica_groups=mesh['rep'=96,'fsdp'=8] {'rep'}, dimensions={0}, use_global_device_ids=true | all-gather | bytes 297984 | tf_op jit(solution)/shard_map/all_gather | solution.py:71
  162.6 22.6 %select_reduce_fusion = f32[2,12,32,128]{3,2,1,0:T(8,128)S(1)} fusion(f32[96,2,12,32]{3,2,1,0:T(8,128)S(1)} %bitcast.45, s32[96,2,12,32]{3,2,1,0:T(8,128)S(1)} %copy.83), kind=kLoop, calls=%fused_computation | loop fusion | flops 28213248 | bytes 983040 | tf_op jit(solution)/shard_map/reduce_sum | solution.py:73
  185.1 0.2 reshape_reshape.2
  185.4 0.9 fusion.10
  186.3 0.9 convolution_bitcast_fusion
  187.2 0.5 copy.94
  187.7 1.0 reshape.59
  (27 shorter events, 0.5 us)
Async XLA Ops:
  7.2 60.7 %reduce-scatter.2.cloned.1.call-start = ((), (), s32[]{:S(2)}) async-start(), calls=%async_computation.1 | async-start | bytes 3538944 | tf_op jit(solution)/shard_map/reduce_scatter | solution.py:58
  9.1 1.9 copy-start.1
  11.0 1.0 copy-start
  69.3 1.9 copy-start.2
  69.4 1.9 copy-start.4
  69.4 1.9 copy-start.6
  76.6 4.4 %copy-start.3 = (f32[2,12,32]{2,1,0:T(8,128)S(1)}, f32[2,12,32]{2,1,0:T(8,128)}, u32[]{:S(2)}) copy-start(f32[2,12,32]{2,1,0:T(8,128)} %copy.84) | copy-start | bytes 9220
  81.0 104.3 %copy-start.5 = (f32[64]{0:T(128)S(1)}, f32[64]{0:T(128)}, u32[]{:S(2)}) copy-start(f32[64]{0:T(128)} %get-tuple-element.12) | copy-start | bytes 772
  81.0 104.3 %copy-start.7 = (f32[64]{0:T(128)S(1)}, f32[64]{0:T(128)}, u32[]{:S(2)}) copy-start(f32[64]{0:T(128)} %get-tuple-element.13) | copy-start | bytes 772
Sparse Core Ops, SparseCore 0:
  11.2 56.6 reduce-scatter.1
where the time goes:
time: 196 us
  blocking collectives  81.5 us (42%)
  waiting for transfers between devices  52.5 us (27%)
  other arithmetic  26.6 us (14%)
  between operations  14.3 us (7%)
  local copies, waits for them, and re-layouts  11.5 us (6%)
  matrix products  9.06 us (5%)
    all_gather x1, blocking collectives, shards(): lax.all_gather(kept[None], 'rep', axis=0, tiled=True)[..., None]  81.5 us
    reduce_scatter x1, waiting for transfers between devices, shards(): lax.psum_scatter(grads.astype(jnp.float32), 'fsdp', scatter_dimension=3,...  52.5 us
    reduce_sum x1, other arithmetic, shards(): gathered = jnp.sum(placed, axis=0)  22.6 us
    dot_general x4, matrix products, inverse_transform(): jnp.einsum('ij,acil,lk->acjk', table, spectra, table, precision=lax.Preci...  6.58 us
    unnamed x21, local copies, waits for them, and re-layouts  4.78 us
  transfers between devices with their start and end apart: 1, of which 1 were waited for; matrix products, arithmetic and copies ran while one was open for 2% of the time, Pallas kernels for 0%

commit v1 on v0

v1 whole, which is shorter than its diff:
```python
import functools

import jax
import jax.numpy as jnp
import numpy as np
from jax import lax
from jax.experimental import pallas as pl
from jax.experimental.pallas import tpu as pltpu
from jax.sharding import PartitionSpec as P

SPAN = 64
KEEP = 32
LANES = 128
SPACING = SPAN * SPAN // KEEP
CROSS = 8
DECAY = 0.999
MESH = pl.DeviceIdType.MESH


def tables():
    freq = np.arange(SPAN)[:, None]
    sample = np.arange(SPAN)[None, :]
    c = np.cos(np.pi * (2.0 * sample + 1.0) * freq / (2.0 * SPAN))
    c = c * np.where(freq == 0, np.sqrt(1.0 / SPAN), np.sqrt(2.0 / SPAN))
    pair = np.kron(np.eye(2), c)
    halves = [np.kron(np.eye(4), c[i1::2].T) for i1 in range(2)]
    rows_forward = np.concatenate(halves, axis=1)
    halves = [np.tile(np.kron(np.eye(2), c[i1::2].T), (1, 2)) for i1 in range(2)]
    rows_inverse = np.concatenate(halves, axis=1)
    return [t.astype(np.float32) for t in (pair, rows_forward, rows_inverse)]


def split_table(table, axis):
    high = table.astype(jnp.bfloat16)
    low = (table - high.astype(jnp.float32)).astype(jnp.bfloat16)
    return jnp.concatenate([high, high, low], axis=axis)


def split_value(value, axis):
    high = value.astype(jnp.bfloat16)
    low = (value - high.astype(jnp.float32)).astype(jnp.bfloat16)
    return jnp.concatenate([high, low, high], axis=axis)


def dot_nn(a, b):
    return lax.dot_general(a, b, (((1,), (0,)), ((), ())), preferred_element_type=jnp.float32)


def dot_nt(a, b):
    return lax.dot_general(a, b, (((1,), (1,)), ((), ())), preferred_element_type=jnp.float32)


def kernel(
    n_rep, n_ring, pieces, schedule,
    grads_hbm, momentum_hbm, indices_hbm, pair_hbm, rows_forward_hbm, rows_inverse_hbm,
    remaining_hbm, update_hbm,
    grads, momentum, indices, pair, rows_forward, rows_inverse, pair_f, rows_f, rows_i, pair_i,
    first, partial, offsets, fresh, own, kept_all, remaining, update,
    load_sem, chunk_sem, send_sem, recv_sem, z_send, z_recv, x_send, x_recv, out_sem,
):
    width = pieces * LANES
    depth = n_rep // CROSS
    half = SPAN
    rep = lax.axis_index("rep")
    me = lax.axis_index("fsdp")
    z = rep // CROSS
    cross = rep % CROSS
    ring = [lax.rem(me + 1, n_ring), lax.rem(me + n_ring - 1, n_ring)]
    z_peers = [lax.rem(z + d, depth) * CROSS + cross for d in range(1, depth)]
    x_peers = [z * CROSS + lax.rem(cross + d, CROSS) for d in range(1, CROSS)]

    distances = [4, 3, -3, 2, -2, 1, -1, 0]
    chunk_loads = {}
    for slot, distance in enumerate(distances):
        start = pl.multiple_of(lax.rem(me + distance + n_ring, n_ring) * width, LANES)
        columns = pl.ds(start, width)
        chunk_loads[distance] = pltpu.make_async_copy(
            grads_hbm.at[:, columns], grads.at[slot], chunk_sem.at[slot]
        )
        chunk_loads[distance].start()
    loads = [
        pltpu.make_async_copy(source, target, load_sem.at[slot])
        for slot, (source, target) in enumerate(
            [
                (indices_hbm, indices), (pair_hbm, pair), (rows_forward_hbm, rows_forward),
                (rows_inverse_hbm, rows_inverse), (momentum_hbm, momentum),
            ]
        )
    ]
    for load in loads:
        load.start()

    barrier = pltpu.get_barrier_semaphore()
    for neighbour in ring:
        pl.semaphore_signal(barrier, inc=1, device_id=(rep, neighbour), device_id_type=MESH)
    for peer in z_peers + x_peers:
        pl.semaphore_signal(barrier, inc=1, device_id=(peer, me), device_id_type=MESH)

    def own_part(distance, piece, rows=slice(None)):
        slot = distances.index(distance)
        return grads[slot, rows, piece * LANES : (piece + 1) * LANES].astype(jnp.float32)

    def hop(way, step, piece):
        if step == 1:
            rows = pl.ds(0, half) if way == 0 else pl.ds(half, half)
            source = first.at[piece, rows]
            target = partial.at[way, 0, piece, rows]
        else:
            source = partial.at[way, step - 2, piece]
            target = partial.at[way, step - 1, piece]
        return pltpu.make_async_remote_copy(
            src_ref=source,
            dst_ref=target,
            send_sem=send_sem.at[way, step - 1, piece],
            recv_sem=recv_sem.at[way, step - 1, piece],
            device_id=(rep, ring[way]),
            device_id_type=MESH,
        )

    chunk_loads[4].wait()
    for piece in range(pieces):
        first[piece] = own_part(4, piece)
    pl.semaphore_wait(barrier, 2 + len(z_peers) + len(x_peers))

    waited = {4}

    def need(distance):
        if distance not in waited:
            chunk_loads[distance].wait()
            waited.add(distance)

    def send_first(piece):
        for way in range(2):
            hop(way, 1, piece).start()
        need(3)
        need(-3)
        partial[0, 0, piece, half:] = own_part(3, piece, slice(half, None))
        partial[1, 0, piece, :half] = own_part(-3, piece, slice(0, half))

    def send_on(step, piece):
        for way in range(2):
            distance = (5 - step) * (1 if way == 0 else -1)
            need(distance)
            hop(way, step - 1, piece).wait_recv()
            if step == 2:
                rows = slice(0, half) if way == 0 else slice(half, None)
            else:
                rows = slice(None)
            partial[way, step - 2, piece, rows] += own_part(distance, piece, rows)
            hop(way, step, piece).start()

    offset_axis = lax.broadcasted_iota(jnp.int32, (LANES, LANES), 0)
    low_lanes = lax.broadcasted_iota(jnp.int32, (SPAN, 2 * LANES), 1) % LANES < SPAN

    def prepare(piece):
        if piece == 0:
            for load in loads:
                load.wait()
            pair_f[...] = split_table(pair[...], 1)
            rows_f[...] = split_table(rows_forward[...], 0)
            rows_i[...] = split_table(rows_inverse[...], 1)
            pair_i[...] = split_table(pair[...], 0)
        rows = [indices[a, 2 * piece + c] for c in range(2) for a in range(2)]
        positions = jnp.concatenate(rows, axis=0)
        offsets[piece, :n_rep] = jnp.transpose(positions & (SPACING - 1))

    def inverse(spectra):
        wide = jnp.concatenate([spectra[:SPAN], spectra[SPAN:]], axis=1)
        stacked = jnp.concatenate(
            [jnp.where(low_lanes, wide, 0.0), jnp.where(low_lanes, 0.0, wide)], axis=0
        )
        half_way = dot_nt(rows_i[...], split_value(stacked, 1))
        return dot_nn(split_value(half_way, 1), pair_i[...])

    def gather_z(piece, peer):
        row = kept_all.at[piece, cross, z]
        return pltpu.make_async_remote_copy(
            src_ref=row,
            dst_ref=row,
            send_sem=z_send.at[piece],
            recv_sem=z_recv.at[piece],
            device_id=(peer, me),
            device_id_type=MESH,
        )

    def gather_x(piece, peer):
        rows = kept_all.at[piece, cross]
        return pltpu.make_async_remote_copy(
            src_ref=rows,
            dst_ref=rows,
            send_sem=x_send.at[piece],
            recv_sem=x_recv.at[piece],
            device_id=(peer, me),
            device_id_type=MESH,
        )

    def wait_z(piece, sem):
        rows = kept_all.at[piece, 0, pl.ds(0, depth - 1)]
        pltpu.make_async_copy(rows, rows, sem.at[piece]).wait()

    def wait_x(piece, sem):
        rows = kept_all.at[piece, pl.ds(0, CROSS - 1)]
        pltpu.make_async_copy(rows, rows, sem.at[piece]).wait()

    def finish(piece):
        need(0)
        for way in range(2):
            hop(way, 4, piece).wait_recv()
        columns = slice(piece * LANES, (piece + 1) * LANES)
        gradient = own_part(0, piece) + partial[0, 3, piece] + partial[1, 3, piece]
        value = DECAY * momentum[:, columns] + gradient
        fresh[piece] = value
        step = dot_nt(pair_f[...], split_value(value, 1))
        step = jnp.concatenate([step[:SPAN], step[SPAN:]], axis=1)
        step = dot_nn(split_value(step, 1), rows_f[...])
        spectra = jnp.concatenate([step[:, :LANES], step[:, LANES:]], axis=0)
        chosen = jnp.where(offset_axis == offsets[piece, pl.ds(rep, 1)], spectra, 0.0)
        kept_all[piece, cross, z] = jnp.sum(chosen, axis=0, keepdims=True)
        for peer in z_peers:
            gather_z(piece, peer).start()
        own[piece] = chosen

    def subtract(piece):
        columns = slice(piece * LANES, (piece + 1) * LANES)
        remaining[:, columns] = fresh[piece] - inverse(own[piece])

    def pass_on(piece):
        wait_z(piece, z_recv)
        for peer in x_peers:
            gather_x(piece, peer).start()

    def place(piece):
        wait_x(piece, x_recv)

        def add_rows(row, total):
            base = pl.multiple_of(row * CROSS, CROSS)
            for member in range(CROSS):
                position = offsets[piece, pl.ds(base, CROSS)][member : member + 1]
                value = kept_all[piece, member, row]
                total = total + jnp.where(offset_axis == position, value, 0.0)
            return total

        total = lax.fori_loop(0, depth, add_rows, jnp.zeros((LANES, LANES), jnp.float32))
        columns = slice(piece * LANES, (piece + 1) * LANES)
        update[:, columns] = inverse(total)

    stages = {
        "first": send_first, "prepare": prepare, "finish": finish, "subtract": subtract,
        "pass": pass_on, "place": place,
    }
    for stage, piece in schedule:
        if isinstance(stage, int):
            send_on(stage, piece)
        else:
            stages[stage](piece)

    outs = [
        pltpu.make_async_copy(remaining, remaining_hbm, out_sem.at[0]),
        pltpu.make_async_copy(update, update_hbm, out_sem.at[1]),
    ]
    for out in outs:
        out.start()
    for piece in range(pieces):
        for way in range(2):
            for step in range(1, 5):
                hop(way, step, piece).wait_send()
        wait_z(piece, z_send)
        wait_x(piece, x_send)
    for out in outs:
        out.wait()


def order():
    return (
        [("first", p) for p in (0, 1, 2)]
        + [("prepare", p) for p in range(6)]
        + [(s, p) for s in (2, 3, 4) for p in (0, 1, 2)]
        + [("first", p) for p in (3, 4, 5)]
        + [
            ("finish", 0), (2, 3), ("finish", 1), (2, 4), ("pass", 0), ("finish", 2), (2, 5),
            ("pass", 1), ("subtract", 0), (3, 3), ("pass", 2), ("place", 0), (3, 4), ("subtract", 1), ("place", 1),
            (3, 5), ("subtract", 2), (4, 3), ("place", 2), (4, 4), (4, 5),
            ("finish", 3), ("subtract", 3), ("finish", 4), ("pass", 3), ("subtract", 4), ("finish", 5), ("pass", 4),
            ("place", 3), ("pass", 5), ("subtract", 5), ("place", 4), ("place", 5),
        ]
    )


def solution(mesh):
    n_rep, n_ring = mesh.shape["rep"], mesh.shape["fsdp"]
    consts = tables()

    def shards(grads, momentum, indices):
        rows, total_width = grads.shape[2:]
        width = momentum.shape[2]
        pieces = width // LANES
        positions = jnp.transpose(indices, (1, 2, 3, 0))
        grads2, momentum2 = grads.reshape(rows, total_width), momentum.reshape(rows, width)
        f32, bf16 = jnp.float32, jnp.bfloat16
        tile = (LANES, LANES)
        dma = pltpu.SemaphoreType.DMA
        remaining, update = pl.pallas_call(
            functools.partial(kernel, n_rep, n_ring, pieces, order()),
            out_shape=[jax.ShapeDtypeStruct((rows, width), f32)] * 2,
            in_specs=[pl.BlockSpec(memory_space=pl.ANY)] * 6,
            out_specs=[pl.BlockSpec(memory_space=pl.ANY)] * 2,
            scratch_shapes=[
                pltpu.VMEM((n_ring, rows, width), bf16),
                pltpu.VMEM((rows, width), f32),
                pltpu.VMEM(positions.shape, jnp.int32),
                *[pltpu.VMEM(c.shape, f32) for c in consts],
                pltpu.VMEM((LANES, 3 * LANES), bf16),
                pltpu.VMEM((6 * LANES, 2 * LANES), bf16),
                pltpu.VMEM((LANES, 6 * LANES), bf16),
                pltpu.VMEM((3 * LANES, LANES), bf16),
                pltpu.VMEM((pieces, *tile), f32),
                pltpu.VMEM((2, 4, pieces, *tile), f32),
                pltpu.VMEM((pieces, *tile), jnp.int32),
                pltpu.VMEM((pieces, *tile), f32),
                pltpu.VMEM((pieces, *tile), f32),
                pltpu.VMEM((pieces, CROSS, n_rep // CROSS, 1, LANES), f32),
                pltpu.VMEM((rows, width), f32),
                pltpu.VMEM((rows, width), f32),
                dma((5,)),
                dma((n_ring,)),
                dma((2, 4, pieces)),
                dma((2, 4, pieces)),
                dma((pieces,)),
                dma((pieces,)),
                dma((pieces,)),
                dma((pieces,)),
                dma((2,)),
            ],
            compiler_params=pltpu.CompilerParams(
                collective_id=0, has_side_effects=True, vmem_limit_bytes=60 * 2**20
            ),
        )(grads2, momentum2, positions, *[jnp.asarray(c) for c in consts])
        return remaining[None], update

    in_specs = (P("rep", "fsdp", None, None), P("rep", None, "fsdp"), P(None, None, "fsdp", None))
    out_specs = (P("rep", None, "fsdp"), P(None, "fsdp"))
    return jax.shard_map(shards, mesh=mesh, in_specs=in_specs, out_specs=out_specs, check_vma=False)
```

time: 196 us -> 80.6 us (0.41)
  blocking collectives: 81.5 us -> 0 us
  Pallas kernels: 0 us -> 76.2 us
  waiting for transfers between devices: 52.5 us -> 0 us
  other arithmetic: 26.6 us -> 0 us
  between operations: 14.3 us -> 0.64 us
  matrix products: 9.06 us -> 0 us
  local copies, waits for them, and re-layouts: 11.5 us -> 3.53 us
    all_gather x1 -> x0, blocking collectives: 81.5 us -> none  [shards(): lax.all_gather(kept[None], 'rep', axis=0, tiled=True)[..., None]]
    pallas_call x0 -> x1, Pallas kernels: none -> 76.2 us  [shards(): pl.pallas_call(functools.partial(kernel, n_rep, n_ring, pieces, order()),...]
    reduce_scatter x1 -> x0, waiting for transfers between devices: 52.5 us -> none  [shards(): lax.psum_scatter(grads.astype(jnp.float32), 'fsdp', scatter_dimension=3,...]
    reduce_sum x2 -> x0, other arithmetic: 22.7 us -> none  [the longest x1 22.6 us: shards(): gathered = jnp.sum(placed, axis=0)]
    dot_general x6 -> x0, matrix products: 9.06 us -> none  [the longest x4 6.58 us: inverse_transform(): jnp.einsum('ij,acil,lk->acjk', table, spectra, table, precision=lax.Preci...]
    unnamed x21 -> x2, local copies, waits for them, and re-layouts: 4.78 us -> 3.53 us
  transfers between devices with their start and end apart: 1 -> 0, of which waited for: 1 -> 0; matrix products, arithmetic and copies ran while one was open for 2% -> 0% of each run, Pallas kernels for 0% -> 0%
where the time goes in v1:
time: 80.6 us; the launch traced here: 80.3 us
  Pallas kernels  76.2 us (95%)
  local copies, waits for them, and re-layouts  3.53 us (4%)
    pallas_call x1, Pallas kernels, shards(): pl.pallas_call(functools.partial(kernel, n_rep, n_ring, pieces, order()),...  76.2 us
    unnamed x2, local copies, waits for them, and re-layouts  3.53 us

profile of v1, /device:TPU:1, one launch (start us, length us, event | category | flops | bytes accessed | tf_op | source)
XLA Modules:
  0.0 80.3 jit_solution(1042469622497250085)
XLA Ops:
  0.6 76.2 %shard_map.77 = (f32[128,768]{1,0:T(8,128)}, f32[128,768]{1,0:T(8,128)}) custom-call(bf16[128,6144]{1,0:T(8,128)(2,1)} %bitcast.4, f32[128,768]{1,0:T(8,128)} %bitcast.6, s32[2,12,32,96]{3,2,1,0:T(8,128)} %bitcast.7, f32[128,128]{1,0:T(8,128)} %constant.6.clone.pair_hbm, f32[256,256]{1,0:T(8,128)} %constant.7.clone.rows_forward_hbm, ...), custom_call_target="tpu_custom_call" | custom-call | tf_op jit(solution)/shard_map/pallas_call | solution.py:302
  76.8 1.8 %copy.10 = f32[1,128,768]{2,1,0:T(8,128)} copy(f32[1,128,768]{2,1,0:T(8,128)} %bitcast.5) | data formatting | bytes 786432
  78.6 1.8 %copy.11 = f32[128,768]{1,0:T(8,128)} copy(f32[128,768]{1,0:T(8,128)} %get-tuple-element.9) | data formatting | bytes 786432

commit v2 on v1

v2 whole, which is shorter than its diff:
```python
import functools

import jax
import jax.numpy as jnp
import numpy as np
from jax import lax
from jax.experimental import pallas as pl
from jax.experimental.pallas import tpu as pltpu
from jax.sharding import PartitionSpec as P

SPAN = 64
KEEP = 32
LANES = 128
SPACING = SPAN * SPAN // KEEP
CORES = 2
CROSS = 8
DECAY = 0.999
MESH = pl.DeviceIdType.MESH


def tables():
    freq = np.arange(SPAN)[:, None]
    sample = np.arange(SPAN)[None, :]
    c = np.cos(np.pi * (2.0 * sample + 1.0) * freq / (2.0 * SPAN))
    c = c * np.where(freq == 0, np.sqrt(1.0 / SPAN), np.sqrt(2.0 / SPAN))
    pair = np.kron(np.eye(2), c)
    rows = np.concatenate([np.kron(np.eye(2), c[i1::2].T) for i1 in range(2)], axis=1)
    return [t.astype(np.float32) for t in (pair, rows)]


def halves(value):
    high = value.astype(jnp.bfloat16)
    return high, (value - high.astype(jnp.float32)).astype(jnp.bfloat16)


def split_table(table, axis):
    high, low = halves(table)
    return jnp.concatenate([high, high, low], axis=axis)


def split_value(value, axis):
    high, low = halves(value)
    return jnp.concatenate([high, low, high], axis=axis)


def dot_nn(a, b):
    return lax.dot_general(a, b, (((1,), (0,)), ((), ())), preferred_element_type=jnp.float32)


def dot_nt(a, b):
    return lax.dot_general(a, b, (((1,), (1,)), ((), ())), preferred_element_type=jnp.float32)


def kernel(
    n_rep, n_ring, pieces, schedule,
    grads_hbm, momentum_hbm, indices_hbm, pair_hbm, rows_hbm,
    remaining, update,
    grads, momentum, indices, pair, rows, pair_b, pair_f, rows_f, rows_i, pair_i,
    first, partial, offsets, chosen_at, spectra, kept_part, kept_in, kept_own, kept_all,
    load_sem, chunk_sem, send_sem, recv_sem, index_sem, part_sem, z_send, z_recv, x_send, x_recv, update_send, update_recv,
):
    width = pieces * LANES
    depth = n_rep // CROSS
    half = SPAN
    group = pieces // CORES
    rep = lax.axis_index("rep")
    me = lax.axis_index("fsdp")
    z = rep // CROSS
    x = rep % CROSS // CORES
    core = rep % CORES
    chips = CROSS // CORES
    z_peers = [(lax.rem(z + d, depth), lax.rem(core + e, CORES)) for e in range(CORES) for d in range(depth)][1:]
    z_devices = [(to * CROSS + x * CORES + side, me) for to, side in z_peers]
    x_devices = [(z * CROSS + lax.rem(x + d, chips) * CORES + core, me) for d in range(1, chips)]
    other_core = (rep + 1 - 2 * core, me)

    distances = [4, 3, -3, 2, -2, 1, -1, 0]
    last = n_ring - 1
    holder = [lax.rem(me + d + n_ring, n_ring) for d in distances]
    ring = [holder[distances.index(1)], holder[distances.index(-1)]]

    chunk_loads = {}
    for slot, distance in enumerate(distances):
        columns = pl.ds(pl.multiple_of(holder[slot] * width, LANES), width)
        chunk_loads[distance] = pltpu.make_async_copy(
            grads_hbm.at[:, columns], grads.at[slot], chunk_sem.at[slot]
        )
    loads = [
        pltpu.make_async_copy(source, target, load_sem.at[slot])
        for slot, (source, target) in enumerate(
            [
                (indices_hbm, indices), (pair_hbm, pair), (rows_hbm, rows), (momentum_hbm, momentum),
            ]
        )
    ]
    chunk_loads[4].start()
    loads[0].start()
    for distance in distances[1:]:
        chunk_loads[distance].start()
    for load in loads[1:]:
        load.start()

    barrier = pltpu.get_barrier_semaphore()
    for neighbour in holder[:last]:
        pl.semaphore_signal(barrier, inc=1, device_id=(rep, neighbour), device_id_type=MESH)
    for device in z_devices + x_devices:
        pl.semaphore_signal(barrier, inc=1, device_id=device, device_id_type=MESH)

    def own_part(distance, piece, rows=slice(None)):
        slot = distances.index(distance)
        return grads[slot, rows, piece * LANES : (piece + 1) * LANES].astype(jnp.float32)

    def hop(way, step, piece):
        if step == 1:
            rows = pl.ds(0, half) if way == 0 else pl.ds(half, half)
            source = first.at[piece, rows]
            target = partial.at[way, 0, piece, rows]
        else:
            source = partial.at[way, step - 2, piece]
            target = partial.at[way, step - 1, piece]
        return pltpu.make_async_remote_copy(
            src_ref=source,
            dst_ref=target,
            send_sem=send_sem.at[way, step - 1, piece],
            recv_sem=recv_sem.at[way, step - 1, piece],
            device_id=(rep, ring[way]),
            device_id_type=MESH,
        )

    waited = set()

    def need(distance):
        if distance not in waited:
            chunk_loads[distance].wait()
            waited.add(distance)

    need(4)
    for piece in range(pieces):
        first[piece] = own_part(4, piece)
    pl.semaphore_wait(barrier, last + len(z_devices) + len(x_devices))

    def send_first(piece):
        for way in range(2):
            hop(way, 1, piece).start()

    def fill_half(piece):
        need(3)
        need(-3)
        partial[0, 0, piece, half:] = own_part(3, piece, slice(half, None))
        partial[1, 0, piece, :half] = own_part(-3, piece, slice(0, half))

    def send_on(step, piece):
        for way in range(2):
            distance = (5 - step) * (1 if way == 0 else -1)
            need(distance)
            hop(way, step - 1, piece).wait_recv()
            if step == 2:
                rows = slice(0, half) if way == 0 else slice(half, None)
            else:
                rows = slice(None)
            partial[way, step - 2, piece, rows] += own_part(distance, piece, rows)
            hop(way, step, piece).start()

    offset_axis = lax.broadcasted_iota(jnp.int32, (LANES, LANES), 0)
    column_axis = lax.broadcasted_iota(jnp.int32, (LANES, LANES), 0) % SPAN
    low = lax.broadcasted_iota(jnp.int32, (1, LANES), 1) < SPAN
    low_tile = lax.broadcasted_iota(jnp.int32, (SPAN, LANES), 1) < SPAN

    def prepare(piece):
        if piece == 0:
            loads[0].wait()
        parts = [indices[a, 2 * piece + c] for c in range(2) for a in range(2)]
        positions = jnp.concatenate(parts, axis=0)
        offsets[piece, :n_rep] = jnp.transpose(positions & (SPACING - 1))
        line = offsets[piece, pl.ds(rep, 1)]
        turned = pltpu.roll(line, SPAN, 1)
        chosen_at[me, piece, 0] = jnp.where(low, line, turned - SPAN)
        chosen_at[me, piece, 1] = jnp.where(low, turned, line - SPAN)

    def split_tables(_):
        for load in loads[1:]:
            load.wait()
        table = pair[...]
        pair_b[...] = jnp.concatenate(halves(table), axis=1)
        pair_f[...] = split_table(table, 1)
        pair_i[...] = split_table(table, 0)
        high, rest = halves(rows[...])
        rows_f[:LANES] = jnp.concatenate([high, rest], axis=1)
        rows_f[LANES:] = jnp.concatenate([high, jnp.zeros_like(rest)], axis=1)
        rows_i[...] = jnp.concatenate([high, high, rest], axis=1)

    def exchange(ref, sem, slot, row):
        source, target = row
        return pltpu.make_async_remote_copy(
            src_ref=ref[0].at[source],
            dst_ref=ref[1].at[target],
            send_sem=sem.at[0],
            recv_sem=sem.at[1],
            device_id=(rep, holder[slot]),
            device_id_type=MESH,
        )

    def wait_rows(ref, sem):
        rows = ref.at[pl.ds(0, last)]
        pltpu.make_async_copy(rows, rows, sem).wait()

    def send_indices(_):
        for slot in range(last):
            exchange((chosen_at, chosen_at), index_sem, slot, (me, me)).start()

    def along_rows(lines):
        both = dot_nn(jnp.concatenate(halves(lines), axis=1), rows_f[...])
        return both[:, :LANES] + both[:, LANES:]

    def forward(value):
        return along_rows(dot_nt(pair_f[...], split_value(value, 1)))

    def transform(slot):
        need(distances[slot])
        if slot == last:
            for piece in range(pieces):
                columns = slice(piece * LANES, (piece + 1) * LANES)
                spectra[slot, piece] = forward(DECAY * momentum[:, columns] + own_part(0, piece))
            return
        lines = []
        for piece in range(0, pieces, 2):
            parts = [grads[slot, :, q * LANES : (q + 1) * LANES] for q in (piece, piece + 1)]
            parts = jnp.concatenate(parts, axis=0)
            step = dot_nt(pair_b[...], jnp.concatenate([parts, parts], axis=1))
            lines += [step[:, :LANES], step[:, LANES:]]
        spectra[slot] = along_rows(jnp.concatenate(lines, axis=0)).reshape(pieces, LANES, LANES)

    def pick(slot, piece, values):
        at = chosen_at[holder[slot], piece]
        both = jnp.concatenate([jnp.broadcast_to(at[c], (SPAN, LANES)) for c in range(2)], axis=0)
        return jnp.where(column_axis == both, values, 0.0)

    def choose(_):
        wait_rows(chosen_at, index_sem.at[1])
        for slot in range(n_ring):
            for piece in range(pieces):
                chosen = pick(slot, piece, spectra[slot, piece])
                sums = [jnp.sum(chosen[c * SPAN : (c + 1) * SPAN], axis=0, keepdims=True) for c in range(2)]
                sums = [line + pltpu.roll(line, SPAN, 1) for line in sums]
                kept_part[slot, piece] = jnp.where(low, sums[0], sums[1])
            if slot < last:
                exchange((kept_part, kept_in), part_sem, slot, (slot, slot)).start()

    def gather_z(side, device):
        return pltpu.make_async_remote_copy(
            src_ref=kept_own.at[side],
            dst_ref=kept_all.at[:, x, z * CORES + core],
            send_sem=z_send,
            recv_sem=z_recv,
            device_id=device,
            device_id_type=MESH,
        )

    def gather_x(piece, device):
        rows = kept_all.at[piece, x]
        return pltpu.make_async_remote_copy(
            src_ref=rows,
            dst_ref=rows,
            send_sem=x_send.at[piece],
            recv_sem=x_recv.at[piece],
            device_id=device,
            device_id_type=MESH,
        )

    def wait_z(sem):
        rows = kept_all.at[:, 0, pl.ds(0, len(z_devices))]
        pltpu.make_async_copy(rows, rows, sem).wait()

    def wait_x(piece, sem):
        rows = kept_all.at[piece, pl.ds(0, chips - 1)]
        pltpu.make_async_copy(rows, rows, sem.at[piece]).wait()

    def swap(piece):
        start = pl.multiple_of((core * group + piece) * LANES, LANES)
        columns = update.at[:, pl.ds(start, LANES)]
        return pltpu.make_async_remote_copy(
            src_ref=columns,
            dst_ref=columns,
            send_sem=update_send.at[piece],
            recv_sem=update_recv.at[piece],
            device_id=other_core,
            device_id_type=MESH,
        )

    def sum_kept(_):
        wait_rows(kept_in, part_sem.at[1])
        for piece in range(pieces):
            total = kept_part[last, piece]
            for slot in range(last):
                total = total + kept_in[slot, piece]
            kept_own[piece // group, piece % group] = total
        for (_, side), device in zip(z_peers, z_devices):
            gather_z(side, device).start()
        for piece in range(group):
            kept_all[piece, x, z * CORES + core] = kept_own[core, piece]

    def pass_on(_):
        wait_z(z_recv)
        for piece in range(group):
            for device in x_devices:
                gather_x(piece, device).start()

    def inverse(wanted):
        half_way = dot_nt(rows_i[...], split_value(wanted, 1))
        return dot_nn(split_value(half_way, 1), pair_i[...])

    def place(piece):
        wait_x(piece, x_recv)
        piece_at = core * group + piece

        def add_rows(row, total):
            base = pl.multiple_of(row * CROSS, CROSS)
            for member in range(CROSS):
                position = offsets[piece_at, pl.ds(base, CROSS)][member : member + 1]
                value = kept_all[piece, member // CORES, row * CORES + member % CORES]
                total = total + jnp.where(offset_axis == position, value, 0.0)
            return total

        total = lax.fori_loop(0, depth, add_rows, jnp.zeros((LANES, LANES), jnp.float32))
        top, bottom = total[:SPAN], total[SPAN:]
        swapped = [
            jnp.where(low_tile, top, pltpu.roll(bottom, SPAN, 1)),
            jnp.where(low_tile, pltpu.roll(top, SPAN, 1), bottom),
        ]
        columns = pl.ds(pl.multiple_of(piece_at * LANES, LANES), LANES)
        update[:, columns] = inverse(jnp.concatenate(swapped, axis=0))
        swap(piece).start()

    def finish(piece):
        for way in range(2):
            hop(way, 4, piece).wait_recv()
        columns = slice(piece * LANES, (piece + 1) * LANES)
        gradient = own_part(0, piece) + partial[0, 3, piece] + partial[1, 3, piece]
        value = DECAY * momentum[:, columns] + gradient
        remaining[:, columns] = value - inverse(pick(last, piece, forward(value)))

    stages = {
        "first": send_first, "fill": fill_half, "prepare": prepare, "tables": split_tables,
        "indices": send_indices, "transform": transform, "choose": choose, "sum": sum_kept,
        "pass": pass_on, "place": place, "finish": finish,
    }
    for stage, piece in schedule:
        if isinstance(stage, int):
            send_on(stage, piece)
        else:
            stages[stage](piece)

    for piece in range(pieces):
        for way in range(2):
            for step in range(1, 5):
                hop(way, step, piece).wait_send()
    wait_rows(chosen_at, index_sem.at[0])
    wait_rows(kept_part, part_sem.at[0])
    wait_z(z_send)
    for piece in range(group):
        wait_x(piece, x_send)
        swap(piece).wait()


def order():
    def on(step, *which):
        return [(step, p) for p in which]

    return (
        on("first", 0, 1, 2) + on("prepare", 0, 1, 2, 3, 4, 5) + [("indices", 0)] + on("first", 3, 4, 5)
        + on("fill", 0, 1, 2, 3, 4, 5)
        + [("tables", 0)] + on("transform", 0, 1) + on(2, 0, 1) + on("transform", 2, 3) + on(2, 2, 3)
        + on("transform", 4, 5) + on(2, 4, 5) + on("transform", 6, 7)
        + [("choose", 0)] + on(3, 0, 1, 2, 3) + [("sum", 0)] + on(3, 4, 5) + on(4, 0, 1)
        + [("pass", 0)] + on(4, 2, 3)
        + on("place", 0) + on(4, 4) + on("place", 1) + on(4, 5) + on("place", 2)
        + on("finish", 0, 1, 2, 3, 4, 5)
    )


def solution(mesh):
    n_rep, n_ring = mesh.shape["rep"], mesh.shape["fsdp"]
    consts = tables()

    def shards(grads, momentum, indices):
        rows, total_width = grads.shape[2:]
        width = momentum.shape[2]
        pieces = width // LANES
        positions = jnp.transpose(indices, (1, 2, 3, 0))
        grads2, momentum2 = grads.reshape(rows, total_width), momentum.reshape(rows, width)
        f32, bf16 = jnp.float32, jnp.bfloat16
        tile = (LANES, LANES)
        dma = pltpu.SemaphoreType.DMA
        remaining, update = pl.pallas_call(
            functools.partial(kernel, n_rep, n_ring, pieces, order()),
            out_shape=[pltpu.VMEM((rows, width), f32)] * 2,
            in_specs=[pl.BlockSpec(memory_space=pl.ANY)] * 5,
            out_specs=[pl.BlockSpec(memory_space=pltpu.VMEM)] * 2,
            scratch_shapes=[
                pltpu.VMEM((n_ring, rows, width), bf16),
                pltpu.VMEM((rows, width), f32),
                pltpu.VMEM(positions.shape, jnp.int32),
                *[pltpu.VMEM(c.shape, f32) for c in consts],
                pltpu.VMEM((LANES, 2 * LANES), bf16),
                pltpu.VMEM((LANES, 3 * LANES), bf16),
                pltpu.VMEM((2 * LANES, 2 * LANES), bf16),
                pltpu.VMEM((LANES, 3 * LANES), bf16),
                pltpu.VMEM((3 * LANES, LANES), bf16),
                pltpu.VMEM((pieces, *tile), f32),
                pltpu.VMEM((2, 4, pieces, *tile), f32),
                pltpu.VMEM((pieces, *tile), jnp.int32),
                pltpu.VMEM((n_ring, pieces, 2, 1, LANES), jnp.int32),
                pltpu.VMEM((n_ring, pieces, *tile), f32),
                pltpu.VMEM((n_ring, pieces, 1, LANES), f32),
                pltpu.VMEM((n_ring, pieces, 1, LANES), f32),
                pltpu.VMEM((CORES, pieces // CORES, 1, LANES), f32),
                pltpu.VMEM((pieces // CORES, CROSS // CORES, n_rep // CROSS * CORES, 1, LANES), f32),
                dma((4,)),
                dma((n_ring,)),
                dma((2, 4, pieces)),
                dma((2, 4, pieces)),
                dma((2,)),
                dma((2,)),
                dma(()),
                dma(()),
                *[dma((pieces // CORES,))] * 4,
            ],
            compiler_params=pltpu.CompilerParams(
                collective_id=0, has_side_effects=True, vmem_limit_bytes=58 * 2**20
            ),
        )(grads2, momentum2, positions, *[jnp.asarray(c) for c in consts])
        return remaining[None], update

    in_specs = (P("rep", "fsdp", None, None), P("rep", None, "fsdp"), P(None, None, "fsdp", None))
    out_specs = (P("rep", None, "fsdp"), P(None, "fsdp"))
    return jax.shard_map(shards, mesh=mesh, in_specs=in_specs, out_specs=out_specs, check_vma=False)
```

time: 80.6 us -> 59 us (0.73)
  Pallas kernels: 76.2 us -> 56.7 us
  local copies, waits for them, and re-layouts: 3.53 us -> 1.49 us
    pallas_call x1, Pallas kernels: 76.2 us -> 56.7 us  [shards(): pl.pallas_call(functools.partial(kernel, n_rep, n_ring, pieces, order()),...]
    unnamed x2, local copies, waits for them, and re-layouts: 3.53 us -> 1.49 us
where the time goes in v2:
time: 59 us; the launch traced here: 58.9 us
  Pallas kernels  56.7 us (96%)
  local copies, waits for them, and re-layouts  1.49 us (3%)
  between operations  0.64 us (1%)
    pallas_call x1, Pallas kernels, shards(): pl.pallas_call(functools.partial(kernel, n_rep, n_ring, pieces, order()),...  56.7 us
    unnamed x2, local copies, waits for them, and re-layouts  1.49 us

profile of v2, /device:TPU:1, one launch (start us, length us, event | category | flops | bytes accessed | tf_op | source)
XLA Modules:
  0.0 58.9 jit_solution(4569233773533537652)
XLA Ops:
  0.6 56.7 %shard_map.68 = (f32[128,768]{1,0:T(8,128)S(1)}, f32[128,768]{1,0:T(8,128)S(1)}) custom-call(bf16[128,6144]{1,0:T(8,128)(2,1)} %bitcast.5, f32[128,768]{1,0:T(8,128)} %bitcast.6, s32[2,12,32,96]{3,2,1,0:T(8,128)} %bitcast.7, f32[128,128]{1,0:T(8,128)} %constant.4.clone.pair_hbm, f32[128,128]{1,0:T(8,128)} %constant.5.clone.rows_hbm), custom_call_target="tpu_custom_call" | custom-call | tf_op jit(solution)/shard_map/pallas_call | solution.py:394
  57.4 0.7 %copy.9 = f32[1,128,768]{2,1,0:T(8,128)} copy(f32[1,128,768]{2,1,0:T(8,128)S(1)} %bitcast.4) | data formatting | bytes 786432
  58.1 0.7 %copy.10 = f32[128,768]{1,0:T(8,128)} copy(f32[128,768]{1,0:T(8,128)S(1)} %get-tuple-element.7) | data formatting | bytes 786432

commit v3 on v2

--- a/solution.py
+++ b/solution.py
@@ -134,10 +134,11 @@
             chunk_loads[distance].wait()
             waited.add(distance)
 
-    need(4)
-    for piece in range(pieces):
-        first[piece] = own_part(4, piece)
-    pl.semaphore_wait(barrier, last + len(z_devices) + len(x_devices))
+    def enter(_):
+        need(4)
+        for piece in range(pieces):
+            first[piece] = own_part(4, piece)
+        pl.semaphore_wait(barrier, last + len(z_devices) + len(x_devices))
 
     def send_first(piece):
         for way in range(2):
@@ -172,10 +173,7 @@
         parts = [indices[a, 2 * piece + c] for c in range(2) for a in range(2)]
         positions = jnp.concatenate(parts, axis=0)
         offsets[piece, :n_rep] = jnp.transpose(positions & (SPACING - 1))
-        line = offsets[piece, pl.ds(rep, 1)]
-        turned = pltpu.roll(line, SPAN, 1)
-        chosen_at[me, piece, 0] = jnp.where(low, line, turned - SPAN)
-        chosen_at[me, piece, 1] = jnp.where(low, turned, line - SPAN)
+        chosen_at[me, piece] = offsets[piece, pl.ds(rep, 1)]
 
     def split_tables(_):
         for load in loads[1:]:
@@ -217,22 +215,24 @@
 
     def transform(slot):
         need(distances[slot])
-        if slot == last:
-            for piece in range(pieces):
-                columns = slice(piece * LANES, (piece + 1) * LANES)
-                spectra[slot, piece] = forward(DECAY * momentum[:, columns] + own_part(0, piece))
-            return
         lines = []
         for piece in range(0, pieces, 2):
             parts = [grads[slot, :, q * LANES : (q + 1) * LANES] for q in (piece, piece + 1)]
             parts = jnp.concatenate(parts, axis=0)
-            step = dot_nt(pair_b[...], jnp.concatenate([parts, parts], axis=1))
+            if slot == last:
+                old = [momentum[:, q * LANES : (q + 1) * LANES] for q in (piece, piece + 1)]
+                value = DECAY * jnp.concatenate(old, axis=0) + parts.astype(jnp.float32)
+                step = dot_nt(pair_f[...], split_value(value, 1))
+            else:
+                step = dot_nt(pair_b[...], jnp.concatenate([parts, parts], axis=1))
             lines += [step[:, :LANES], step[:, LANES:]]
         spectra[slot] = along_rows(jnp.concatenate(lines, axis=0)).reshape(pieces, LANES, LANES)
 
     def pick(slot, piece, values):
-        at = chosen_at[holder[slot], piece]
-        both = jnp.concatenate([jnp.broadcast_to(at[c], (SPAN, LANES)) for c in range(2)], axis=0)
+        line = chosen_at[holder[slot], piece]
+        turned = pltpu.roll(line, SPAN, 1)
+        at = [jnp.where(low, line, turned - SPAN), jnp.where(low, turned, line - SPAN)]
+        both = jnp.concatenate([jnp.broadcast_to(row, (SPAN, LANES)) for row in at], axis=0)
         return jnp.where(column_axis == both, values, 0.0)
 
     def choose(_):
@@ -340,7 +340,7 @@
         remaining[:, columns] = value - inverse(pick(last, piece, forward(value)))
 
     stages = {
-        "first": send_first, "fill": fill_half, "prepare": prepare, "tables": split_tables,
+        "enter": enter, "first": send_first, "fill": fill_half, "prepare": prepare, "tables": split_tables,
         "indices": send_indices, "transform": transform, "choose": choose, "sum": sum_kept,
         "pass": pass_on, "place": place, "finish": finish,
     }
@@ -367,14 +367,12 @@
         return [(step, p) for p in which]
 
     return (
-        on("first", 0, 1, 2) + on("prepare", 0, 1, 2, 3, 4, 5) + [("indices", 0)] + on("first", 3, 4, 5)
-        + on("fill", 0, 1, 2, 3, 4, 5)
-        + [("tables", 0)] + on("transform", 0, 1) + on(2, 0, 1) + on("transform", 2, 3) + on(2, 2, 3)
-        + on("transform", 4, 5) + on(2, 4, 5) + on("transform", 6, 7)
-        + [("choose", 0)] + on(3, 0, 1, 2, 3) + [("sum", 0)] + on(3, 4, 5) + on(4, 0, 1)
-        + [("pass", 0)] + on(4, 2, 3)
-        + on("place", 0) + on(4, 4) + on("place", 1) + on(4, 5) + on("place", 2)
-        + on("finish", 0, 1, 2, 3, 4, 5)
+        on("prepare", 0, 1, 2, 3, 4, 5) + [("tables", 0), ("enter", 0), ("indices", 0)]
+        + on("first", 0, 1, 2, 3, 4, 5) + on("fill", 0, 1, 2, 3, 4, 5)
+        + on("transform", 0, 1, 2, 3) + on(2, 0, 1) + on("transform", 4, 5, 6, 7)
+        + [("choose", 0)] + on(2, 2, 3, 4, 5) + [("sum", 0)] + on(3, 0, 1, 2, 3, 4, 5)
+        + [("pass", 0)] + on(4, 0, 1, 2, 3, 4, 5)
+        + on("place", 0, 1, 2) + on("finish", 0, 1, 2, 3, 4, 5)
     )
 
 
@@ -409,7 +407,7 @@
                 pltpu.VMEM((pieces, *tile), f32),
                 pltpu.VMEM((2, 4, pieces, *tile), f32),
                 pltpu.VMEM((pieces, *tile), jnp.int32),
-                pltpu.VMEM((n_ring, pieces, 2, 1, LANES), jnp.int32),
+                pltpu.VMEM((n_ring, pieces, 1, LANES), jnp.int32),
                 pltpu.VMEM((n_ring, pieces, *tile), f32),
                 pltpu.VMEM((n_ring, pieces, 1, LANES), f32),
                 pltpu.VMEM((n_ring, pieces, 1, LANES), f32),

time: 59 us -> 54.1 us (0.917)
  Pallas kernels: 56.7 us -> 51.8 us
    pallas_call x1, Pallas kernels: 56.7 us -> 51.8 us  [shards(): pl.pallas_call(functools.partial(kernel, n_rep, n_ring, pieces, order()),...]
where the time goes in v3:
time: 54.1 us; the launch traced here: 53.9 us
  Pallas kernels  51.8 us (96%)
  local copies, waits for them, and re-layouts  1.49 us (3%)
  between operations  0.64 us (1%)
    pallas_call x1, Pallas kernels, shards(): pl.pallas_call(functools.partial(kernel, n_rep, n_ring, pieces, order()),...  51.8 us
    unnamed x2, local copies, waits for them, and re-layouts  1.49 us

profile of v3, /device:TPU:1, one launch (start us, length us, event | category | flops | bytes accessed | tf_op | source)
XLA Modules:
  0.0 53.9 jit_solution(11126675394428083678)
XLA Ops:
  0.6 51.8 %shard_map.68 = (f32[128,768]{1,0:T(8,128)S(1)}, f32[128,768]{1,0:T(8,128)S(1)}) custom-call(bf16[128,6144]{1,0:T(8,128)(2,1)} %bitcast.5, f32[128,768]{1,0:T(8,128)} %bitcast.6, s32[2,12,32,96]{3,2,1,0:T(8,128)} %bitcast.7, f32[128,128]{1,0:T(8,128)} %constant.4.clone.pair_hbm, f32[128,128]{1,0:T(8,128)} %constant.5.clone.rows_hbm), custom_call_target="tpu_custom_call" | custom-call | tf_op jit(solution)/shard_map/pallas_call | solution.py:392
  52.4 0.7 %copy.9 = f32[1,128,768]{2,1,0:T(8,128)} copy(f32[1,128,768]{2,1,0:T(8,128)S(1)} %bitcast.4) | data formatting | bytes 786432
  53.2 0.7 %copy.10 = f32[128,768]{1,0:T(8,128)} copy(f32[128,768]{1,0:T(8,128)S(1)} %get-tuple-element.7) | data formatting | bytes 786432

commit v4 on v3

--- a/solution.py
+++ b/solution.py
@@ -57,7 +57,7 @@
     remaining, update,
     grads, momentum, indices, pair, rows, pair_b, pair_f, rows_f, rows_i, pair_i,
     first, partial, offsets, chosen_at, spectra, kept_part, kept_in, kept_own, kept_all,
-    load_sem, chunk_sem, send_sem, recv_sem, index_sem, part_sem, z_send, z_recv, x_send, x_recv, update_send, update_recv,
+    load_sem, chunk_sem, send_sem, recv_sem, index_sem, part_sem, z_send, z_recv, x_send, x_recv, update_send, update_recv, up_sem, ready_sem,
 ):
     width = pieces * LANES
     depth = n_rep // CROSS
@@ -69,8 +69,10 @@
     x = rep % CROSS // CORES
     core = rep % CORES
     chips = CROSS // CORES
-    z_peers = [(lax.rem(z + d, depth), lax.rem(core + e, CORES)) for e in range(CORES) for d in range(depth)][1:]
-    z_devices = [(to * CROSS + x * CORES + side, me) for to, side in z_peers]
+    def along_z(to):
+        return [(to * CROSS + x * CORES + side, me) for side in range(CORES)]
+
+    above, below = along_z(jnp.minimum(z + 1, depth - 1)), along_z(jnp.maximum(z - 1, 0))
     x_devices = [(z * CROSS + lax.rem(x + d, chips) * CORES + core, me) for d in range(1, chips)]
     other_core = (rep + 1 - 2 * core, me)
 
@@ -93,18 +95,29 @@
             ]
         )
     ]
+    loads[0].start()
     chunk_loads[4].start()
-    loads[0].start()
+    for load in loads[1:3]:
+        load.start()
     for distance in distances[1:]:
         chunk_loads[distance].start()
-    for load in loads[1:]:
-        load.start()
+    loads[3].start()
 
     barrier = pltpu.get_barrier_semaphore()
     for neighbour in holder[:last]:
         pl.semaphore_signal(barrier, inc=1, device_id=(rep, neighbour), device_id_type=MESH)
-    for device in z_devices + x_devices:
+    for device in x_devices + [other_core]:
         pl.semaphore_signal(barrier, inc=1, device_id=device, device_id_type=MESH)
+
+    @pl.when(z > 0)
+    def _():
+        for device in below:
+            pl.semaphore_signal(barrier, inc=1, device_id=device, device_id_type=MESH)
+
+    @pl.when(z < depth - 1)
+    def _():
+        for device in above:
+            pl.semaphore_signal(barrier, inc=1, device_id=device, device_id_type=MESH)
 
     def own_part(distance, piece, rows=slice(None)):
         slot = distances.index(distance)
@@ -138,7 +151,26 @@
         need(4)
         for piece in range(pieces):
             first[piece] = own_part(4, piece)
-        pl.semaphore_wait(barrier, last + len(z_devices) + len(x_devices))
+        neighbours = CORES * (jnp.minimum(z, 1) + jnp.minimum(depth - 1 - z, 1))
+        pl.semaphore_wait(barrier, last + len(x_devices) + 1 + neighbours)
+
+    def announce(_):
+        @pl.when(z > 0)
+        def _():
+            pl.semaphore_wait(up_sem, CORES)
+
+        @pl.when(z < depth - 1)
+        def _():
+            for device in above:
+                pl.semaphore_signal(up_sem, inc=1, device_id=device, device_id_type=MESH)
+
+        for step in range(1, depth):
+
+            @pl.when(z >= step)
+            def _():
+                for device in along_z(z - step):
+                    pl.semaphore_signal(ready_sem, inc=1, device_id=device, device_id_type=MESH)
+
 
     def send_first(piece):
         for way in range(2):
@@ -268,7 +300,7 @@
         )
 
     def wait_z(sem):
-        rows = kept_all.at[:, 0, pl.ds(0, len(z_devices))]
+        rows = kept_all.at[:, 0, pl.ds(0, CORES * depth - 1)]
         pltpu.make_async_copy(rows, rows, sem).wait()
 
     def wait_x(piece, sem):
@@ -294,10 +326,28 @@
             for slot in range(last):
                 total = total + kept_in[slot, piece]
             kept_own[piece // group, piece % group] = total
-        for (_, side), device in zip(z_peers, z_devices):
-            gather_z(side, device).start()
+        for step in range(1, depth):
+
+            @pl.when(z >= step)
+            def _():
+                for side, device in enumerate(along_z(z - step)):
+                    gather_z(side, device).start()
+
+        gather_z(1 - core, other_core).start()
         for piece in range(group):
             kept_all[piece, x, z * CORES + core] = kept_own[core, piece]
+
+    def send_up(_):
+        @pl.when(z < depth - 1)
+        def _():
+            pl.semaphore_wait(ready_sem, CORES * (depth - 1 - z))
+
+        for step in range(1, depth):
+
+            @pl.when(z + step < depth)
+            def _():
+                for side, device in enumerate(along_z(z + step)):
+                    gather_z(side, device).start()
 
     def pass_on(_):
         wait_z(z_recv)
@@ -340,7 +390,7 @@
         remaining[:, columns] = value - inverse(pick(last, piece, forward(value)))
 
     stages = {
-        "enter": enter, "first": send_first, "fill": fill_half, "prepare": prepare, "tables": split_tables,
+        "enter": enter, "announce": announce, "up": send_up, "first": send_first, "fill": fill_half, "prepare": prepare, "tables": split_tables,
         "indices": send_indices, "transform": transform, "choose": choose, "sum": sum_kept,
         "pass": pass_on, "place": place, "finish": finish,
     }
@@ -367,12 +417,13 @@
         return [(step, p) for p in which]
 
     return (
-        on("prepare", 0, 1, 2, 3, 4, 5) + [("tables", 0), ("enter", 0), ("indices", 0)]
-        + on("first", 0, 1, 2, 3, 4, 5) + on("fill", 0, 1, 2, 3, 4, 5)
-        + on("transform", 0, 1, 2, 3) + on(2, 0, 1) + on("transform", 4, 5, 6, 7)
+        [("enter", 0)] + on("first", 0, 1, 2) + on("prepare", 0, 1, 2, 3, 4, 5) + [("indices", 0)]
+        + on("first", 3, 4, 5) + on("fill", 0, 1, 2, 3, 4, 5)
+        + [("tables", 0)] + on("transform", 0, 1) + [("announce", 0)] + on("transform", 2, 3) + on(2, 0, 1)
+        + on("transform", 4, 5, 6, 7)
         + [("choose", 0)] + on(2, 2, 3, 4, 5) + [("sum", 0)] + on(3, 0, 1, 2, 3, 4, 5)
-        + [("pass", 0)] + on(4, 0, 1, 2, 3, 4, 5)
-        + on("place", 0, 1, 2) + on("finish", 0, 1, 2, 3, 4, 5)
+        + [("up", 0)] + on(4, 0, 1, 2, 3, 4, 5) + [("pass", 0)]
+        + on("finish", 0, 1, 2) + on("place", 0, 1, 2) + on("finish", 3, 4, 5)
     )
 
 
@@ -422,6 +473,8 @@
                 dma(()),
                 dma(()),
                 *[dma((pieces // CORES,))] * 4,
+                pltpu.SemaphoreType.REGULAR,
+                pltpu.SemaphoreType.REGULAR,
             ],
             compiler_params=pltpu.CompilerParams(
                 collective_id=0, has_side_effects=True, vmem_limit_bytes=58 * 2**20

time: 54.1 us -> 50.3 us (0.930)
  Pallas kernels: 51.8 us -> 48 us
    pallas_call x1, Pallas kernels: 51.8 us -> 48 us  [shards(): pl.pallas_call(functools.partial(kernel, n_rep, n_ring, pieces, order()),...]
where the time goes in v4:
time: 50.3 us; the launch traced here: 50.1 us
  Pallas kernels  48 us (95%)
  local copies, waits for them, and re-layouts  1.49 us (3%)
  between operations  0.64 us (1%)
    pallas_call x1, Pallas kernels, shards(): pl.pallas_call(functools.partial(kernel, n_rep, n_ring, pieces, order()),...  48 us
    unnamed x2, local copies, waits for them, and re-layouts  1.49 us

profile of v4, /device:TPU:1, one launch (start us, length us, event | category | flops | bytes accessed | tf_op | source)
XLA Modules:
  0.0 50.1 jit_solution(11778526596976099536)
XLA Ops:
  0.6 48.0 %shard_map.68 = (f32[128,768]{1,0:T(8,128)S(1)}, f32[128,768]{1,0:T(8,128)S(1)}) custom-call(bf16[128,6144]{1,0:T(8,128)(2,1)} %bitcast.5, f32[128,768]{1,0:T(8,128)} %bitcast.6, s32[2,12,32,96]{3,2,1,0:T(8,128)} %bitcast.7, f32[128,128]{1,0:T(8,128)} %constant.4.clone.pair_hbm, f32[128,128]{1,0:T(8,128)} %constant.5.clone.rows_hbm), custom_call_target="tpu_custom_call" | custom-call | tf_op jit(solution)/shard_map/pallas_call | solution.py:443
  48.6 0.7 %copy.9 = f32[1,128,768]{2,1,0:T(8,128)} copy(f32[1,128,768]{2,1,0:T(8,128)S(1)} %bitcast.4) | data formatting | bytes 786432
  49.4 0.7 %copy.10 = f32[128,768]{1,0:T(8,128)} copy(f32[128,768]{1,0:T(8,128)S(1)} %get-tuple-element.7) | data formatting | bytes 786432

commit v5 on v4

--- a/solution.py
+++ b/solution.py
@@ -208,7 +208,7 @@
         chosen_at[me, piece] = offsets[piece, pl.ds(rep, 1)]
 
     def split_tables(_):
-        for load in loads[1:]:
+        for load in loads[1:3]:
             load.wait()
         table = pair[...]
         pair_b[...] = jnp.concatenate(halves(table), axis=1)
@@ -247,6 +247,8 @@
 
     def transform(slot):
         need(distances[slot])
+        if slot == last:
+            loads[3].wait()
         lines = []
         for piece in range(0, pieces, 2):
             parts = [grads[slot, :, q * LANES : (q + 1) * LANES] for q in (piece, piece + 1)]
@@ -417,13 +419,13 @@
         return [(step, p) for p in which]
 
     return (
-        [("enter", 0)] + on("first", 0, 1, 2) + on("prepare", 0, 1, 2, 3, 4, 5) + [("indices", 0)]
-        + on("first", 3, 4, 5) + on("fill", 0, 1, 2, 3, 4, 5)
-        + [("tables", 0)] + on("transform", 0, 1) + [("announce", 0)] + on("transform", 2, 3) + on(2, 0, 1)
-        + on("transform", 4, 5, 6, 7)
-        + [("choose", 0)] + on(2, 2, 3, 4, 5) + [("sum", 0)] + on(3, 0, 1, 2, 3, 4, 5)
-        + [("up", 0)] + on(4, 0, 1, 2, 3, 4, 5) + [("pass", 0)]
-        + on("finish", 0, 1, 2) + on("place", 0, 1, 2) + on("finish", 3, 4, 5)
+        on("prepare", 0, 1, 2, 3, 4, 5) + [("tables", 0), ("enter", 0), ("indices", 0)]
+        + on("first", 0, 1, 2, 3, 4, 5) + on("fill", 0, 1, 2, 3, 4, 5)
+        + on("transform", 0, 1) + [("announce", 0)] + on("transform", 2, 3) + on(2, 0, 1)
+        + on("transform", 4, 5, 6, 7) + [("choose", 0)] + on(2, 2, 3, 4, 5)
+        + [("sum", 0)] + on(3, 0, 1, 2, 3, 4, 5)
+        + [("up", 0)] + on(4, 0, 1, 2, 3) + [("pass", 0)] + on(4, 4, 5)
+        + on("finish", 0, 1) + on("place", 0, 1, 2) + on("finish", 2, 3, 4, 5)
     )
 
 
@@ -480,6 +482,22 @@
                 collective_id=0, has_side_effects=True, vmem_limit_bytes=58 * 2**20
             ),
         )(grads2, momentum2, positions, *[jnp.asarray(c) for c in consts])
+
+        def copy_out(a, b, c, d, sems):
+            one = pltpu.make_async_copy(a, c, sems.at[0])
+            two = pltpu.make_async_copy(b, d, sems.at[1])
+            one.start()
+            two.start()
+            one.wait()
+            two.wait()
+
+        remaining, update = pl.pallas_call(
+            copy_out,
+            out_shape=[jax.ShapeDtypeStruct((rows, width), f32)] * 2,
+            in_specs=[pl.BlockSpec(memory_space=pltpu.VMEM)] * 2,
+            out_specs=[pl.BlockSpec(memory_space=pl.ANY)] * 2,
+            scratch_shapes=[dma((2,))],
+        )(*[pltpu.with_memory_space_constraint(v, pltpu.VMEM) for v in (remaining, update)])
         return remaining[None], update
 
     in_specs = (P("rep", "fsdp", None, None), P("rep", None, "fsdp"), P(None, None, "fsdp", None))

time: 50.3 us -> 49.1 us (0.976)
  local copies, waits for them, and re-layouts: 1.49 us -> 0 us
    unnamed x2 -> x0, local copies, waits for them, and re-layouts: 1.49 us -> none
    pallas_call x0 -> x1, Pallas kernels: none -> 0.89 us  [shards(): pl.pallas_call(copy_out, out_shape=[jax.ShapeDtypeStruct((rows, width), f...]
    pallas_call x1, Pallas kernels: 48 us -> 47.3 us  [shards(): pl.pallas_call(functools.partial(kernel, n_rep, n_ring, pieces, order()),...]
where the time goes in v5:
time: 49.1 us; the launch traced here: 48.9 us
  Pallas kernels  48.2 us (98%)
  between operations  0.64 us (1%)
    pallas_call x1, Pallas kernels, shards(): pl.pallas_call(functools.partial(kernel, n_rep, n_ring, pieces, order()),...  47.3 us

profile of v5, /device:TPU:1, one launch (start us, length us, event | category | flops | bytes accessed | tf_op | source)
XLA Modules:
  0.0 48.9 jit_solution(17885692727683337423)
XLA Ops:
  0.6 47.3 %shard_map.68 = (f32[128,768]{1,0:T(8,128)S(1)}, f32[128,768]{1,0:T(8,128)S(1)}) custom-call(bf16[128,6144]{1,0:T(8,128)(2,1)} %bitcast.4, f32[128,768]{1,0:T(8,128)} %bitcast.5, s32[2,12,32,96]{3,2,1,0:T(8,128)} %bitcast.6, f32[128,128]{1,0:T(8,128)} %constant.4.clone.pair_hbm, f32[128,128]{1,0:T(8,128)} %constant.5.clone.rows_hbm), custom_call_target="tpu_custom_call" | custom-call | tf_op jit(solution)/shard_map/pallas_call | solution.py:445
  48.0 0.9 %shard_map.69 = (f32[128,768]{1,0:T(8,128)}, f32[128,768]{1,0:T(8,128)}) custom-call(f32[128,768]{1,0:T(8,128)S(1)} %get-tuple-element.6.a, f32[128,768]{1,0:T(8,128)S(1)} %get-tuple-element.7.b), custom_call_target="tpu_custom_call" | custom-call | tf_op jit(solution)/shard_map/pallas_call | solution.py:494
